TPU v7x, 32 devices: a whole 2x2x4 slice. The times are simulated.
32 devices in a mesh: dp: 4 (over z), tensor: 4 (over y, core), ctx: 2 (over x).
Axes of the slice: x: 2, y: 2, z: 4, core: 2. Of those that a mesh axis runs over, the one named last changes fastest.
Arguments:
- tokens: bfloat16 [2048, 2048], P('dp', ('tensor', 'ctx')), may hold values from -6 to 6
- targets: bfloat16 [2048, 2048], P('dp', ('tensor', 'ctx')), may hold values from -6 to 6
- ln_gain: bfloat16 [2048], P(('tensor', 'ctx')), may hold values from 0.5 to 1.5
- up_weight: bfloat16 [2048, 2, 4, 1024], P('dp', None, 'ctx', 'tensor'), may hold values from -0.125 to 0.125
- conv_weight: bfloat16 [4, 4, 1024], P(None, 'ctx', 'tensor'), may hold values from -3 to 3
- conv_bias: bfloat16 [4, 1024], P('ctx', 'tensor'), may hold values from -3 to 3
- qkv_weight: bfloat16 [3, 4, 4, 1024], P(None, None, 'ctx', 'tensor'), may hold values from -3 to 3
- gate_weight: bfloat16 [2, 4, 3, 4, 1024], P(None, None, None, 'ctx', 'tensor'), may hold values from -0.0546875 to 0.0546875
- gate_bias: bfloat16 [2, 4], replicated, may hold values from -3 to 5, as said below
- group_gain: bfloat16 [4, 1024], P('ctx', 'tensor'), may hold values from 0.099609375 to 1.8984375
- skip_gain: bfloat16 [4, 1024], P('ctx', 'tensor'), may hold values from 0.099609375 to 1.8984375
- down_weight: bfloat16 [4, 1024, 2048], P('ctx', 'tensor', 'dp'), may hold values from -0.1875 to 0.1875
- lengths: int32 [4, 3], replicated, may hold values from 64 to 256, as said below
- permutation: int32 [2048], replicated, may hold values from 0 to 2047, as said below
- valid: int32 [2048], P('dp'), may hold values from 0 to 1, as said below
Outputs:
- output: bfloat16 [2048, 2048], P('dp', ('tensor', 'ctx'))
- loss: float32 [], replicated
- grad_input: bfloat16 [2048, 2048], P('dp', ('tensor', 'ctx'))
- grad_ln_gain: float32 [2048], P(('tensor', 'ctx'))
- grad_up_weight: float32 [2048, 2, 4, 1024], P('dp', None, 'ctx', 'tensor')
- grad_conv_weight: float32 [4, 4, 1024], P(None, 'ctx', 'tensor')
- grad_conv_bias: float32 [4, 1024], P('ctx', 'tensor')
- grad_qkv_weight: float32 [3, 4, 4, 1024], P(None, None, 'ctx', 'tensor')
- grad_gate_weight: float32 [2, 4, 3, 4, 1024], P(None, None, None, 'ctx', 'tensor')
- grad_gate_bias: float32 [2, 4], replicated
- grad_group_gain: float32 [4, 1024], P('ctx', 'tensor')
- grad_skip_gain: float32 [4, 1024], P('ctx', 'tensor')
- grad_down_weight: float32 [4, 1024, 2048], P('ctx', 'tensor', 'dp')
Inputs may be any that keep to these rules, and one draw needn't show every extreme that they name: `lengths`: in each pack one sequence has exactly 256 tokens and the others between one eighth and one quarter of 512. A permutation of the 2048 slots; the 512 tokens that one index of dp holds in the loader's order go to every pack, exactly 128 to each. `valid`: A 0 or 1 for each token. `gate_bias`: input gate biases (first index 0) lie from -3 to 0, forget gate biases from 1 to 5.
All inputs are finite; a program needn't handle non-finite values.
Results may differ from a plain program's by a relative error of at most 0.014.
The roundings to bfloat16 on the way count: a program that leaves them out, or rounds other values in their place, can miss the bound.
Values may be sent and summed in bfloat16 or wider, within the bound.
A program may use at most 192 MiB of HBM per device.

v0:
```python
import itertools
import types

import jax
import jax.numpy as jnp
from jax import lax
from jax.experimental import pallas as pl
from jax.experimental.pallas import tpu as pltpu
from jax.sharding import PartitionSpec as P

NEG_FILL = -1e30
EPSILON = 1e-05
BF = jnp.bfloat16
F32 = jnp.float32
MESH = pl.DeviceIdType.MESH
VMEM_LIMIT = 62 * 1024 * 1024
LINE = 128
GROUPS = 2
BAND = 2


def mm(a, b):
    return jnp.dot(a, b, preferred_element_type=F32)


def mm_nt(a, b):
    return lax.dot_general(a, b, (((1,), (1,)), ((), ())), preferred_element_type=F32)


def mm_tn(a, b):
    return lax.dot_general(a, b, (((0,), (0,)), ((), ())), preferred_element_type=F32)


def split(v):
    high = v.astype(BF)
    return high, (v - high.astype(F32)).astype(BF)


def root_inverse(v):
    guess = lax.rsqrt(v)
    return guess * (1.5 - 0.5 * v * guess * guess)


def sigmoid(v):
    return 1.0 / (1.0 + jnp.exp(-v))


class Links:
    def __init__(self, send, recv, limit):
        self.send, self.recv, self.limit = send, recv, limit
        self.used, self.open = 0, []

    def make(self, src, dst, peer):
        k = self.used
        self.used += 1
        assert k < self.limit
        copy = pltpu.make_async_remote_copy(
            src_ref=src,
            dst_ref=dst,
            send_sem=self.send.at[k],
            recv_sem=self.recv.at[k],
            device_id=peer,
            device_id_type=MESH,
        )
        return copy

    def go(self, src, dst, peer):
        copy = self.make(src, dst, peer)
        copy.start()
        self.open.append(copy)
        return copy

    def settle(self, copies):
        for copy in copies:
            copy.wait_send()
        self.open = [c for c in self.open if all(c is not done for done in copies)]

    def close(self):
        self.settle(list(self.open))


class Ring:
    def __init__(self, links, hold, part, next_peer, owners):
        self.links, self.hold, self.part = links, hold, part
        self.peer, self.owners = next_peer, owners
        self.flying, self.at = None, 0

    def start(self):
        block = self.hold.at[self.owners[self.at], self.part]
        self.flying = self.links.go(block, block, self.peer)

    def step(self):
        if self.at >= len(self.owners) - 1:
            return False
        if self.flying is None:
            self.start()
        self.flying.wait_recv()
        self.at += 1
        self.flying = None
        if self.at < len(self.owners) - 1:
            self.start()
            return True
        return False

    def last_leg(self):
        while self.at < len(self.owners) - 2:
            self.step()

    def finish(self):
        while self.step():
            pass

    def settle(self):
        self.links.close()


def when(condition, *actions):
    @pl.when(condition)
    def _():
        for action in actions:
            action()


class LineGather:
    def __init__(self, links, hold, m, count):
        self.z, self.count, self.at = m.z, count, 0
        z, last = m.z, count - 1
        self.ways = []
        for d in range(1, count):
            to_right = jnp.maximum(z - (d - 1), 0)
            to_left = jnp.minimum(z + (d - 1), last)
            self.ways.append(
                (
                    (
                        links.make(hold.at[to_right], hold.at[to_right], m.right),
                        (z < last) & (z >= d - 1),
                        z >= d,
                    ),
                    (
                        links.make(hold.at[to_left], hold.at[to_left], m.left),
                        (z > 0) & (z + d - 1 <= last),
                        z + d <= last,
                    ),
                )
            )

    def start(self):
        for copy, sends, _ in self.ways[self.at]:
            when(sends, copy.start)

    def step(self):
        if self.at >= self.count - 1:
            return
        for copy, _, receives in self.ways[self.at]:
            when(receives, copy.wait_recv)
        self.at += 1
        if self.at < self.count - 1:
            self.start()

    def last_leg(self):
        while self.at < self.count - 2:
            self.step()

    def finish(self):
        while self.at < self.count - 1:
            self.step()

    def settle(self):
        for pair in self.ways:
            for copy, sends, _ in pair:
                when(sends, copy.wait_send)


class LineSum:
    def __init__(self, links, part, hold, target, m, count, size):
        self.part, self.hold, self.target = part, hold, target
        self.z, self.count, self.at, self.size = m.z, count, 0, size
        places = (m.z, count - 1 - m.z)
        self.ways = [
            (
                places[way],
                [
                    links.make(hold.at[way, t], hold.at[way, t + 1], peer)
                    for t in range(count - 1)
                ],
            )
            for way, peer in enumerate((m.right, m.left))
        ]

    def step(self):
        t, count = self.at, self.count
        if t > count - 1:
            return
        self.at += 1
        size = self.size
        pieces = self.hold.shape[-2] // size

        def arrive(place, copies):
            if t:
                when((place > 0) & (place <= t), copies[t - 1].wait_recv)

        def lines(j):
            return pl.ds(pl.multiple_of(j * size, size), size)

        def add(way, place, own, j):
            if t:
                own = own + jnp.where(place > 0, self.hold[way, t, lines(j)].astype(F32), 0.0)
            return own

        if t == count - 1:
            for place, copies in self.ways:
                arrive(place, copies)

            def last(j, carry):
                total = self.part(self.z, j)
                for way, (place, _) in enumerate(self.ways):
                    total = add(way, place, total, j)
                self.target(total, lines(j))
                return carry

            lax.fori_loop(0, pieces, last, 0)
            return
        for way, (place, copies) in enumerate(self.ways):
            arrive(place, copies)

            def send(way=way, place=place, copies=copies):
                ahead = count - 1 - t
                owner = self.z + ahead if way == 0 else self.z - ahead

                def piece(j, carry):
                    self.hold[way, t, lines(j)] = add(
                        way, place, self.part(owner, j), j
                    ).astype(BF)
                    return carry

                lax.fori_loop(0, pieces, piece, 0)
                copies[t].start()

            when(place <= t, send)

    def settle(self):
        for place, copies in self.ways:
            for t, copy in enumerate(copies):
                when(place <= t, copy.wait_send)


class RingSum:
    def __init__(self, links, part, hold, target, m, count, size):
        self.links, self.part, self.hold, self.target = links, part, hold, target
        self.m, self.count, self.at = m, count, -1
        self.sent = []

    def step(self):
        if self.at >= self.count - 1:
            return
        self.at += 1
        own = self.part(self.m.owners[(self.at + 1) % self.count])
        if self.at:
            self.sent[-1].wait_recv()
            own = own + self.hold[0, self.at].astype(F32)
        if self.at == self.count - 1:
            self.target(own, pl.ds(0, own.shape[0]))
            return
        self.hold[0, self.at] = own.astype(BF)
        self.sent.append(
            self.links.go(
                self.hold.at[0, self.at], self.hold.at[0, self.at + 1], self.m.ring_next
            )
        )

    def settle(self):
        self.links.settle(self.sent)


def coordinates(dp_count):
    z, t, c = lax.axis_index("dp"), lax.axis_index("tensor"), lax.axis_index("ctx")
    core = lax.rem(t, 2)
    m = types.SimpleNamespace(z=z, t=t, c=c, core=core, y=lax.div(t, 2))
    m.sib_t, m.far_t, m.other_c = t + 1 - 2 * core, lax.rem(t + 2, 4), 1 - c
    m.sib, m.yn, m.xn = (z, m.sib_t, c), (z, m.far_t, c), (z, t, m.other_c)
    m.slot = t * 2 + c
    m.slot_x, m.slot_y, m.slot_d = t * 2 + m.other_c, m.far_t * 2 + c, m.far_t * 2 + m.other_c
    m.to_sib = 2 - 4 * core
    if dp_count == 4:
        def after(v):
            return lax.rem(2 * v + 1, 5)

        def before(v):
            return lax.rem(3 * v + 2, 5)
    else:
        def after(v):
            return lax.rem(v + 1, dp_count)

        def before(v):
            return lax.rem(v + dp_count - 1, dp_count)

    m.ring_next = (after(z), t, c)
    m.owners = [z]
    for _ in range(dp_count - 1):
        m.owners.append(before(m.owners[-1]))
    m.right = (lax.rem(z + 1, dp_count), t, c)
    m.left = (lax.rem(z + dp_count - 1, dp_count), t, c)
    m.dp_peers = [(lax.rem(z + d, dp_count), t, c) for d in range(1, dp_count)]
    m.plane_peers = [
        (z, lax.rem(t + dt, 4), lax.rem(c + dc, 2))
        for dt in range(4)
        for dc in range(2)
        if dt or dc
    ]
    m.tensor_peers = [(z, lax.rem(t + dt, 4), c) for dt in range(1, 4)]
    return m


def plane_gather(links, m, full, rows, base=0):
    half = rows // 2
    first, second, whole = pl.ds(base, half), pl.ds(base + half, half), pl.ds(base, rows)
    sent = []

    def send(slot, part, peer):
        sent.append(links.go(full.at[slot, part], full.at[slot, part], peer))
        return sent[-1]

    x_first = send(m.slot, first, m.xn)
    y_second = send(m.slot, second, m.yn)
    to_sib = send(m.slot, whole, m.sib)
    x_second = send(m.slot, second, m.xn)
    y_first = send(m.slot, first, m.yn)
    yield m.slot
    to_sib.wait_recv()
    yield m.slot + m.to_sib
    x_first.wait_recv()
    d_first = send(m.slot_x, first, m.yn)
    y_second.wait_recv()
    d_second = send(m.slot_y, second, m.xn)
    x_second.wait_recv()
    sib_x = send(m.slot_x, whole, m.sib)
    yield m.slot_x
    y_first.wait_recv()
    sib_y = send(m.slot_y, whole, m.sib)
    yield m.slot_y
    sib_x.wait_recv()
    yield m.slot_x + m.to_sib
    d_first.wait_recv()
    d_second.wait_recv()
    sib_d = send(m.slot_d, whole, m.sib)
    yield m.slot_d
    sib_y.wait_recv()
    yield m.slot_y + m.to_sib
    sib_d.wait_recv()
    yield m.slot_d + m.to_sib
    links.settle(sent)


def idle():
    pass


def to_lanes(columns, rows):
    lane = lax.broadcasted_iota(jnp.int32, (rows, 128), 1)
    out = jnp.zeros((rows, 128), F32)
    for j, column in enumerate(columns):
        out = jnp.where(lane == j, column, out)
    return out.T[:8]


def to_lanes_one(column):
    line = lax.broadcasted_iota(jnp.int32, (8, 128), 0)
    lane = lax.broadcasted_iota(jnp.int32, (8, 128), 1)
    return jnp.sum(jnp.where(line == lane, column, 0.0), axis=0, keepdims=True)


def to_columns(lines):
    rows = lines.shape[1]
    return jnp.concatenate([lines, jnp.zeros((120, rows), F32)], axis=0).T


def push_sum(links, m, lines, box, peers, own_place, count):
    box[own_place] = lines
    copies = [links.go(box.at[own_place], box.at[own_place], peer) for peer in peers]

    def finish():
        for copy in copies:
            copy.wait_recv()
        total = box[0]
        for k in range(1, count):
            total = total + box[k]
        return total

    return finish


def prefix_lanes(v):
    width = v.shape[1]
    lane = lax.broadcasted_iota(jnp.int32, v.shape, 1)
    step = 1
    while step < width:
        v = v + jnp.where(lane >= step, pltpu.roll(v, step, 1), 0.0)
        step *= 2
    return v


def band(rows):
    out, at = [], 0
    for i in range(rows // LINE):
        low = max(0, i - BAND)
        out.append((i, low, at, i - low + 1))
        at += i - low + 1
    return out, at


def wide(ref, h, at, width):
    return jnp.concatenate([ref[h, at + k] for k in range(width)], axis=1)


def plane_scatter(links, m, part, b, rows, services):
    size = rows // GROUPS
    half = size // 2
    own_k = m.y * 2 + m.c
    far_y = 1 - m.y
    links.settle(b.scatter_copies)
    copies = []
    for k in range(4):
        b.out[k] = part(k // 2, 1 - m.core, k % 2).astype(BF)
        for g in range(GROUPS):
            at = pl.ds(g * size, size)
            copies.append(links.go(b.out.at[k, at], b.into.at[k, at], m.sib))

    def own_part(k, carry):
        b.acc[k] = part(lax.div(k, 2), m.core, lax.rem(k, 2))
        return carry

    lax.fori_loop(0, 4, own_part, 0)
    b.scatter_copies = list(copies)
    services[0]()

    def send(g, place, k, at, peer):
        place += 6 * g
        b.small_out[place] = b.acc[k, at].astype(BF)
        copy = links.go(b.small_out.at[place], b.small_in.at[place], peer)
        b.scatter_copies.append(copy)
        return copy

    def receive(g, place, k, at, copy):
        copy.wait_recv()
        b.acc[k, at] += b.small_in[place + 6 * g].astype(F32)

    parts = [(pl.ds(g * size, half), pl.ds(g * size + half, half)) for g in range(GROUPS)]
    second_phase, third_phase = [], []
    for g, (first, second) in enumerate(parts):
        at = pl.ds(g * size, size)
        for k in range(4):
            copies[k * GROUPS + g].wait_recv()
            b.acc[k, at] += b.into[k, at].astype(F32)
        second_phase.append(
            [send(g, y, y * 2 + m.other_c, first, m.xn) for y in range(2)]
            + [send(g, 2 + x, far_y * 2 + x, second, m.yn) for x in range(2)]
        )
    services[1]()
    for g, (first, second) in enumerate(parts):
        flying = second_phase[g]
        for y in range(2):
            receive(g, y, y * 2 + m.c, first, flying[y])
        for x in range(2):
            receive(g, 2 + x, m.y * 2 + x, second, flying[2 + x])
        third_phase.append(
            (
                send(g, 4, far_y * 2 + m.c, first, m.yn),
                send(g, 5, m.y * 2 + m.other_c, second, m.xn),
            )
        )
    services[2]()
    for g, (first, second) in enumerate(parts):
        receive(g, 4, own_k, first, third_phase[g][0])
        receive(g, 5, own_k, second, third_phase[g][1])
        yield g, slice(g * size, (g + 1) * size)


def forward(b, m, links, shape):
    rows, local, chan, n_dp, block, wide_d = shape
    cap, heads = rows // n_dp, local // chan
    width, all_heads = 8 * wide_d, 2 * heads
    scale = (4 * chan) ** -0.5
    blocks, n_blocks = band(rows)
    low_rows = pl.ds(0, rows)

    b.scatter_copies = []
    partners = m.plane_peers + m.dp_peers
    barrier = pltpu.get_barrier_semaphore()
    for peer in partners:
        pl.semaphore_signal(barrier, inc=1, device_id=peer, device_id_type=MESH)
    own_copies = [
        pltpu.make_async_copy(own, hold.at[m.z], b.local_sem.at[k])
        for k, (own, hold) in enumerate(
            ((b.own_cell, b.up_cell), (b.own_gate, b.up_gate), (b.own_down, b.down))
        )
    ]
    for copy in own_copies:
        copy.start()
    own_place = pl.ds(pl.multiple_of(m.z * cap, 16), cap)

    def slots_of(source):
        return b.permutation[pl.ds(pl.multiple_of(source * rows, rows), rows)].reshape(1, rows)

    b.gains[m.slot] = jnp.broadcast_to(b.ln_gain[...].astype(F32).reshape(1, wide_d), (8, wide_d))
    b.valids[m.z] = jnp.broadcast_to(b.valid[...].astype(F32).reshape(1, rows), (8, rows))
    count = block // 2 if block % 256 == 0 else block
    cells = [
        Ring(links, b.up_cell, pl.ds(at, count), m.ring_next, m.owners)
        for at in range(0, block, count)
    ]
    gate = Ring(links, b.up_gate, pl.ds(0, block), m.ring_next, m.owners)
    down = Ring(links, b.down, pl.ds(0, local), m.ring_next, m.owners)
    if n_dp <= 4:
        mixed_ring = LineGather(links, b.mixed_all, m, n_dp)
    else:
        mixed_ring = Ring(links, b.mixed_all, pl.ds(0, rows), m.ring_next, m.owners)
    own_copies[0].wait()
    pl.semaphore_wait(barrier, len(partners))
    cells[0].start()

    digits = rows.bit_length() - 1
    packs = max(8, n_dp)
    own = slots_of(m.z)
    dest = lax.shift_right_logical(own, digits)
    to_pack = lax.broadcasted_iota(jnp.int32, (packs, rows), 0) == dest
    ahead = prefix_lanes(jnp.where(to_pack, 1.0, 0.0))
    rank = jnp.sum(jnp.where(to_pack, ahead, 0.0), axis=0, keepdims=True).astype(jnp.int32) - 1
    line = lax.broadcasted_iota(jnp.int32, (rows, rows), 0)
    b.send_map[...] = jnp.where(line == dest * cap + rank, 1.0, 0.0).astype(BF)
    b.sent_tokens[...] = mm(b.send_map[...], b.tokens[...]).astype(BF)
    b.full[m.slot, own_place] = b.sent_tokens[own_place]

    def exchange(out, into):
        copies = []
        for d, peer in enumerate(m.dp_peers):
            place = pl.ds(pl.multiple_of(lax.rem(m.z + d + 1, n_dp) * cap, 16), cap)
            copies.append(links.go(out.at[place], into.at[own_place], peer))
        return copies

    b.exchange = exchange
    a2a = exchange(b.sent_tokens, b.full.at[m.slot])
    b.token_copies = a2a
    for ring in cells[1:]:
        ring.start()
    one = pl.ds(0, 1)
    gain_copies = [
        links.go(b.gains.at[m.slot], b.gains.at[m.slot], peer) for peer in m.plane_peers
    ]
    valid_copies = [
        links.go(b.valids.at[m.z, one], b.valids.at[m.z, one], peer) for peer in m.dp_peers
    ]
    for copy in own_copies[1:]:
        copy.wait()

    b.wide_f[...] = jnp.zeros((rows, rows), F32)

    def place_source(s, carry):
        perm = slots_of(s)
        mine = lax.shift_right_logical(perm, digits) == m.z
        ahead = prefix_lanes(jnp.broadcast_to(jnp.where(mine, 1.0, 0.0), (8, rows)))[:1]
        at = jnp.where(mine, s * cap + ahead.astype(jnp.int32) - 1, -1)
        slot = perm - m.z * rows
        slots = jnp.where(line == slot, 1.0, 0.0).astype(BF)
        places = jnp.where(line == at, 1.0, 0.0).astype(BF)
        b.wide_f[...] += mm_nt(slots, places)
        return carry

    lax.fori_loop(0, n_dp, place_source, 0)
    b.recv_map[...] = b.wide_f[...].astype(BF)
    for copy in a2a:
        copy.wait_recv()
    cells[0].step()

    b.sums[...] = jnp.zeros((rows, 128), F32)
    b.squares[...] = jnp.zeros((rows, 128), F32)
    arrivals = 0
    for slot in plane_gather(links, m, b.full, rows):
        columns = pl.ds(pl.multiple_of(slot * wide_d, 128), wide_d)

        def place_rows(r, carry, slot=slot, columns=columns):
            at = pl.ds(pl.multiple_of(r * LINE, LINE), LINE)
            x = mm(b.recv_map[at], b.full[slot])
            b.normed[at, columns] = x.astype(BF)
            b.sums[at] += jnp.sum(x, axis=1, keepdims=True)
            b.squares[at] += jnp.sum(x * x, axis=1, keepdims=True)
            return carry

        lax.fori_loop(0, rows // LINE, place_rows, 0)
        arrivals += 1
        if arrivals in (3, 8):
            cells[-1].step()
        if arrivals == 6:
            cells[0].step()
    own_columns = pl.ds(pl.multiple_of(m.slot * wide_d, 128), wide_d)
    b.x_own[...] = b.normed[:, own_columns]
    b.sent_goal[...] = mm(b.send_map[...], b.targets[...]).astype(BF)
    b.goal_places[own_place] = b.sent_goal[own_place]
    for copy in gain_copies:
        copy.wait_recv()

    def normalise(r, carry):
        at = pl.ds(pl.multiple_of(r * 64, 64), 64)
        mean = b.sums[at][:, :1] / width
        var = b.squares[at][:, :1] / width - mean * mean
        rstd = root_inverse(var + EPSILON)
        b.sums[at] = jnp.broadcast_to(mean, (64, 128))
        b.squares[at] = jnp.broadcast_to(rstd, (64, 128))
        for i in range(8):
            x = b.normed[at, i * wide_d : (i + 1) * wide_d].astype(F32)
            x = (x - mean) * rstd * b.gains[i, :1]
            b.normed[at, i * wide_d : (i + 1) * wide_d] = x.astype(BF)
        return carry

    lax.fori_loop(0, rows // 64, normalise, 0)

    def project(hold, rings, target):
        count = block // len(rings)
        for s in range(n_dp):
            owner = m.owners[s]
            for r, ring in enumerate(rings):
                while ring.at < s:
                    ring.step()
                columns = pl.ds(pl.multiple_of(owner * block + r * count, 128), count)
                product = mm(b.normed[:, columns], hold[owner, r * count : (r + 1) * count])
                target[...] = product if s + r == 0 else target[...] + product

    for ring in cells:
        ring.last_leg()
    gate.start()
    down.start()
    project(b.up_cell, cells, b.wide_f)

    for h in range(heads):
        at = slice(h * chan, (h + 1) * chan)
        for j in range(4):
            b.chan_params[j : j + 1, at] = b.conv_weight[j].astype(F32)[h : h + 1]
        for j, ref in ((4, b.conv_bias), (5, b.group_gain), (6, b.skip_gain)):
            b.chan_params[j : j + 1, at] = ref[...].astype(F32)[h : h + 1]
        for s in range(3):
            for i in range(4):
                tap = b.qkv_weight[s, i].astype(F32)[h : h + 1]
                b.maps8[s, h, i : i + 1] = tap
                b.maps8[s, h, i + 4 : i + 5] = tap
            for g in range(2 * all_heads):
                row = b.gate_weight[g // all_heads, g % all_heads, s].astype(F32)[h : h + 1]
                b.gates_f[g : g + 1, s * local + h * chan : s * local + (h + 1) * chan] = row
    b.gates_f[8:] = jnp.zeros((8, 3 * local), F32)
    b.gates_w[...] = b.gates_f[...].astype(BF)
    place = lax.broadcasted_iota(jnp.int32, (rows, 1), 0)
    ends, total = [], 0
    for k in range(b.lengths.shape[1]):
        total = total + b.lengths[m.z, k]
        ends.append(total)
    begin = jnp.zeros((rows, 1), jnp.int32)
    for end in ends:
        begin = jnp.where(place >= end, end, begin)
    b.begin[...] = jnp.broadcast_to(begin, (rows, 128))

    def convolve(i, carry):
        at = pl.ds(pl.multiple_of(i * 128, 128), 128)
        low = b.wide_f[:, at].astype(BF)
        b.branch[:, at] = low
        x = low.astype(F32)
        since = lax.broadcasted_iota(jnp.int32, (rows, 128), 0) - b.begin[...]
        conv = b.chan_params[4:5, at] + b.chan_params[0:1, at] * x
        for j in range(1, 4):
            back = b.chan_params[j : j + 1, at] * pltpu.roll(x, j, 0)
            conv = conv + jnp.where(since >= j, back, 0.0)
        sig = sigmoid(conv)
        act = conv * sig
        b.act[:, at] = act
        b.slope[:, at] = sig + act * (1.0 - sig)
        return carry

    lax.fori_loop(0, local // 128, convolve, 0)
    r_map = lax.broadcasted_iota(jnp.int32, (chan, chan), 0) // 4
    c_map = lax.broadcasted_iota(jnp.int32, (chan, chan), 1) // 4
    same = r_map == c_map
    for s in range(3):
        for h in range(heads):
            base = b.maps8[s, h]
            dense = jnp.broadcast_to(base[None], (chan // 8, 8, chan)).reshape(chan, chan)
            b.maps[s, h] = jnp.where(same, dense, 0.0).astype(BF)
    for h in range(heads):
        at = slice(h * chan, (h + 1) * chan)
        act = b.act[:, at]
        high, rest = split(act)
        least = ((act - high.astype(F32)) - rest.astype(F32)).astype(BF)
        for s in range(2):
            b.qkv[:, s * local + h * chan : s * local + (h + 1) * chan] = (
                mm(high, b.maps[s, h]) + (mm(rest, b.maps[s, h]) + mm(least, b.maps[s, h]))
            ).astype(BF)
        b.qkv[:, 2 * local + h * chan : 2 * local + (h + 1) * chan] = mm(
            b.branch[:, at], b.maps[2, h]
        ).astype(BF)

    pre_part = mm_nt(b.gates_w[...], b.qkv[...])[:8]
    pre_sum = push_sum(links, m, pre_part, b.pre_box, m.plane_peers, m.slot, 8)

    def q_of(h, i):
        return b.qkv[i * LINE : (i + 1) * LINE, h * chan : (h + 1) * chan]

    def k_of(h, low, n):
        return b.qkv[
            low * LINE : (low + n) * LINE, local + h * chan : local + (h + 1) * chan
        ]

    def v_of(h, low, n):
        return b.qkv[
            low * LINE : (low + n) * LINE, 2 * local + h * chan : 2 * local + (h + 1) * chan
        ]

    b.of = (q_of, k_of, v_of)
    for h in range(heads):
        for i, low, at, n in blocks:
            tile = mm_nt(q_of(h, i), k_of(h, low, n))
            for k in range(n):
                b.score_part[h, at + k] = tile[:, k * LINE : (k + 1) * LINE]
    other = links.go(b.score_part.at[1 - m.core], b.score_in.at[0], m.sib)
    b.score_copy = other
    other.wait_recv()
    b.score_sum[...] = b.score_part[m.core] + b.score_in[0]
    far = links.go(b.score_sum, b.score_in.at[1], m.yn)

    line81 = lax.broadcasted_iota(jnp.int32, (8, 1), 0)
    given = b.gate_bias[...].astype(F32)
    bias = jnp.zeros((8, 1), F32)
    for g in range(2):
        for o in range(all_heads):
            bias = jnp.where(line81 == g * all_heads + o, given[g : g + 1, o : o + 1], bias)
    pre = pre_sum() + bias
    b.pre[...] = pre
    line8 = lax.broadcasted_iota(jnp.int32, (8, rows), 0)
    head = m.c * heads + m.core
    in_gate = jnp.sum(jnp.where(line8 == head, pre, 0.0), axis=0, keepdims=True)
    forget = jnp.sum(jnp.where(line8 == head + all_heads, pre, 0.0), axis=0, keepdims=True)
    log_forget = jnp.minimum(forget, 0.0) - jnp.log(1.0 + jnp.exp(-jnp.abs(forget)))
    rising = prefix_lanes(jnp.broadcast_to(log_forget, (8, rows)))
    rise_col = to_columns(rising)
    gate_line = in_gate - rising[:1]
    gate.step()
    for copy in valid_copies:
        copy.wait_recv()
    b.keep[...] = jnp.zeros((rows, 128), F32)

    def take_source(s, carry):
        perm = slots_of(s)
        valid = b.valids[s][:1]
        pack = lax.shift_right_logical(perm, digits)
        lasts = jnp.zeros((1, rows), jnp.int32)
        for p in range(n_dp):
            last = sum(b.lengths[p, k] for k in range(b.lengths.shape[1]))
            lasts = jnp.where(pack == p, last, lasts)
        counted = jnp.where(perm - pack * rows < lasts, valid, 0.0)
        hits = jnp.where(line == perm - m.z * rows, counted, 0.0)
        b.keep[...] += jnp.sum(hits, axis=1, keepdims=True)
        return carry + jnp.sum(counted, axis=1, keepdims=True)

    valid_count = lax.fori_loop(0, n_dp, take_source, jnp.zeros((1, 1), F32))
    keep = b.keep[:, :1]
    far.wait_recv()
    b.score_part[m.core] = b.score_sum[...] + b.score_in[1]
    for i, low, at, n in blocks:
        lines = slice(i * LINE, (i + 1) * LINE)
        t_at = i * LINE + lax.broadcasted_iota(jnp.int32, (LINE, n * LINE), 0)
        s_at = low * LINE + lax.broadcasted_iota(jnp.int32, (LINE, n * LINE), 1)
        allowed = (s_at <= t_at) & (s_at >= b.begin[lines][:, :1])
        logit = jnp.where(
            allowed, rise_col[lines][:, :1] + gate_line[:, low * LINE : (low + n) * LINE], NEG_FILL
        )
        top = jnp.max(logit, axis=1, keepdims=True)
        decay = jnp.where(allowed, jnp.exp(logit - top), 0.0) * scale
        weight = wide(b.score_part, m.core, at, n) * decay
        den = jnp.sum(weight, axis=1, keepdims=True)
        floor = jnp.exp(-top)
        inv = 1.0 / jnp.maximum(jnp.abs(den), floor)
        shares = (weight * inv).astype(BF)
        b.inv[lines] = jnp.broadcast_to(inv, (LINE, 128))
        sign = jnp.where(jnp.abs(den) > floor, jnp.where(den > 0.0, 1.0, -1.0), 0.0)
        b.sign[lines] = jnp.broadcast_to(sign, (LINE, 128))
        for k in range(n):
            b.decay[at + k] = decay[:, k * LINE : (k + 1) * LINE]
            b.weight[at + k] = weight[:, k * LINE : (k + 1) * LINE]
            b.share[m.core, at + k] = shares[:, k * LINE : (k + 1) * LINE]
    shared = links.go(b.share.at[m.core], b.share.at[m.core], m.sib)
    gate.step()
    shared.wait_recv()
    columns = []
    for h in range(heads):
        for i, low, at, n in blocks:
            lines = slice(i * LINE, (i + 1) * LINE)
            b.hidden[lines, h * chan : (h + 1) * chan] = mm(
                wide(b.share, h, at, n), v_of(h, low, n)
            )
        hid = b.hidden[:, h * chan : (h + 1) * chan]
        columns.append(jnp.sum(hid, axis=1, keepdims=True))
        columns.append(jnp.sum(hid * hid, axis=1, keepdims=True))
    moment_sum = push_sum(
        links, m, to_lanes(columns, rows), b.moment_box, m.tensor_peers, m.t, 4
    )
    gate.finish()
    down.step()
    project(b.up_gate, (gate,), b.wide_f)
    moments = to_columns(moment_sum()) / (4 * chan)
    for h in range(heads):
        mean = moments[:, 2 * h : 2 * h + 1]
        rstd = root_inverse(moments[:, 2 * h + 1 : 2 * h + 2] - mean * mean + EPSILON)
        b.head_rstd[h] = jnp.broadcast_to(rstd, (rows, 128))
        b.head_mean[h] = jnp.broadcast_to(mean, (rows, 128))
    down.step()

    def mix(i, carry):
        at = pl.ds(pl.multiple_of(i * 128, 128), 128)
        h = lax.div(i, chan // 128)
        hat = (b.hidden[:, at] - b.head_mean[h]) * b.head_rstd[h]
        b.hidden[:, at] = hat
        low = b.wide_f[:, at].astype(BF)
        b.gate_low[:, at] = low
        g = low.astype(F32)
        inner = hat * b.chan_params[5:6, at] + b.chan_params[6:7, at] * b.act[:, at]
        b.mixed_all[m.z, :, at] = (inner * (g * sigmoid(g))).astype(BF)
        return carry

    lax.fori_loop(0, local // 128, mix, 0)
    down.last_leg()
    goal_copies = exchange(b.sent_goal, b.goal_places)
    mixed_ring.start()
    down.finish()
    piece = min(block, wide_d)

    def down_part(y, core, x):
        slot = (y * 2 + core) * 2 + x
        parts = []
        for k in range(wide_d // piece):
            if block >= 2 * wide_d:
                owner = lax.div((y * 2 + core) * 2 * wide_d, block)
                at = pl.ds(pl.multiple_of(x * wide_d, 128), wide_d)
                parts.append(mm(b.mixed_all[m.z], b.down[owner, :, at]))
            else:
                owner = lax.div(slot * wide_d, block) + k
                parts.append(mm(b.mixed_all[m.z], b.down[owner]))
        return jnp.concatenate(parts, axis=1)

    own_k = m.y * 2 + m.c
    summed = plane_scatter(links, m, down_part, b, rows, (idle, mixed_ring.step, idle))
    loss_sum = jnp.zeros((1, 1), F32)
    b.arriving = []
    size = rows // GROUPS
    for copy in goal_copies:
        copy.wait_recv()
    b.goal[...] = mm(b.recv_map[...], b.goal_places[...]).astype(BF)
    for g, at in summed:
        result = (b.x_own[at].astype(F32) + b.acc[own_k, at]).astype(BF)
        b.result[at] = result
        difference = result.astype(F32) - b.goal[at].astype(F32)
        own_gradient = ((rows * n_dp) / valid_count * keep[at] * difference).astype(BF)
        b.full[m.slot, at] = own_gradient
        arriving = plane_gather(links, m, b.full, size, g * size)
        slot = next(arriving)
        b.arriving.append(itertools.chain([slot], arriving))
        b.own_gradient[at] = own_gradient
        per_row = jnp.sum(difference * difference, axis=1, keepdims=True)
        loss_sum = loss_sum + jnp.sum(keep[at] * 0.5 * per_row, axis=0, keepdims=True)
    b.loss_part[...] = jnp.broadcast_to(loss_sum / valid_count, (8, 128))
    b.mixed_ring = mixed_ring

    b.sent_out[...] = mm_tn(b.recv_map[...], b.result[...]).astype(BF)
    b.home_out[own_place] = b.sent_out[own_place]
    b.home_copies = exchange(b.sent_out, b.home_out)


def backward(b, m, links, shape):
    rows, local, chan, n_dp, block, wide_d = shape
    cap, heads = rows // n_dp, local // chan
    all_heads = 2 * heads
    width, head_width = 8 * wide_d, 4 * chan
    blocks, n_blocks = band(rows)
    q_of, k_of, v_of = b.of
    line8 = lax.broadcasted_iota(jnp.int32, (8, rows), 0)
    head = m.c * heads + m.core

    size = rows // GROUPS
    for turn, slots in enumerate(zip(*b.arriving)):
        for g, slot in enumerate(slots):
            lines = slice(g * size, (g + 1) * size)
            grads = b.full[slot, lines]
            if block >= wide_d:
                ratio = block // wide_d
                at = pl.ds(pl.multiple_of(lax.rem(slot, ratio) * wide_d, 128), wide_d)
                product = mm_nt(grads, b.down[lax.div(slot, ratio), :, at])
            else:
                ratio = wide_d // block
                product = sum(
                    mm_nt(grads[:, k * block : (k + 1) * block], b.down[slot * ratio + k])
                    for k in range(ratio)
                )
            b.wide_f[lines] = product if turn == 0 else b.wide_f[lines] + product
        if turn == 5:
            b.mixed_ring.step()
    for arriving in b.arriving:
        for _ in arriving:
            pass

    per = rows // 8
    own_rows = pl.ds(pl.multiple_of(m.slot * per, 16), per)
    for d in range(n_dp):
        to = m.z if d == 0 else m.dp_peers[d - 1][0]
        if block >= wide_d:
            ratio = block // wide_d
            for k in range(ratio):
                b.cols_out[to, :, k * wide_d : (k + 1) * wide_d] = b.full[to * ratio + k, own_rows]
        else:
            ratio = wide_d // block
            at = pl.ds(pl.multiple_of(lax.rem(to, ratio) * block, 128), block)
            b.cols_out[to] = b.full[lax.div(to, ratio), own_rows, at]
    from_here = pl.ds(pl.multiple_of(m.z * per, 16), per)
    b.cols[m.slot, from_here] = b.cols_out[m.z]
    cols_copies = [
        links.go(b.cols_out.at[peer[0]], b.cols.at[m.slot, from_here], peer)
        for peer in m.dp_peers
    ]

    def sum_down():
        for copy in cols_copies:
            copy.wait_recv()
        b.mixed_ring.finish()
        b.grad_down[...] = jnp.zeros((local, block), F32)
        for slot in plane_gather(links, m, b.cols, n_dp * per):
            at = pl.ds(pl.multiple_of(slot * per, 16), per)
            for p in range(0, n_dp, 4):
                left = jnp.concatenate([b.mixed_all[p + k, at] for k in range(4)], axis=0)
                b.grad_down[...] += mm_tn(left, b.cols[slot, p * per : (p + 4) * per])
            yield

    down_sum = sum_down()

    def advance(steps):
        for _ in range(steps):
            next(down_sum, None)

    def up_ring(grads, hold, g, h):
        at_h = slice(h * chan, (h + 1) * chan)
        size = block // 2 if g else block

        def part(owner, j=None):
            if j is None:
                at = pl.ds(pl.multiple_of(owner * block, 128), block)
            else:
                at = pl.ds(pl.multiple_of(owner * block + j * size, 128), size)
            return mm_tn(b.normed[:, at], grads[:, at_h])

        def keep(total, lines):
            b.grad_up[lines, g, h] = total

        return (LineSum if n_dp <= 4 else RingSum)(
            links, part, hold.at[h], keep, m, n_dp, size
        )

    gates = [up_ring(b.g_gate, b.ring_gate, 1, h) for h in range(heads)]
    cells = [up_ring(b.g_cell, b.ring_cell, 0, h) for h in range(heads)]

    def ticks(rings):
        for _ in range(n_dp):
            for ring in rings:
                yield ring.step()

    gate_ticks, cell_ticks = ticks(gates), ticks(cells)

    def tick(source):
        return lambda: next(source, None)

    def unmix(i, carry):
        at = pl.ds(pl.multiple_of(i * 128, 128), 128)
        gm = b.wide_f[:, at]
        g = b.gate_low[:, at].astype(F32)
        sig = sigmoid(g)
        silu = g * sig
        hat, act = b.hidden[:, at], b.act[:, at]
        group, skip = b.chan_params[5:6, at], b.chan_params[6:7, at]
        inner = hat * group + skip * act
        b.g_gate[:, at] = (gm * inner * (sig + silu * (1.0 - sig))).astype(BF)
        gi = gm * silu
        b.small[5:6, at] = jnp.sum(gi * hat, axis=0, keepdims=True)
        b.small[6:7, at] = jnp.sum(gi * act, axis=0, keepdims=True)
        b.g_act[:, at] = gi * skip
        b.wide_f[:, at] = gi * group
        return carry

    lax.fori_loop(0, local // 128, unmix, 0)
    b.mixed_ring.last_leg()
    next(gate_ticks)
    next(gate_ticks)
    columns = []
    for h in range(heads):
        u = b.wide_f[:, h * chan : (h + 1) * chan]
        columns.append(jnp.sum(u, axis=1, keepdims=True))
        columns.append(
            jnp.sum(u * b.hidden[:, h * chan : (h + 1) * chan], axis=1, keepdims=True)
        )
    u_sum = push_sum(links, m, to_lanes(columns, rows), b.u_box, m.tensor_peers, m.t, 4)
    u_moments = to_columns(u_sum())
    rhos = []
    for h in range(heads):
        at = slice(h * chan, (h + 1) * chan)
        rstd = b.head_rstd[h][:, :1]
        mean_u = u_moments[:, 2 * h : 2 * h + 1] / head_width
        sum_ux = u_moments[:, 2 * h + 1 : 2 * h + 2]
        d_hidden = rstd * (b.wide_f[:, at] - mean_u - b.hidden[:, at] * (sum_ux / head_width))
        b.d_hidden[:, at] = d_hidden.astype(BF)
        rhos.append(sum_ux * (EPSILON * rstd * rstd))
    rho = jnp.where(m.core == 0, rhos[0], rhos[1])
    links.settle([b.score_copy])
    for h in range(heads):
        for i, low, at, n in blocks:
            tile = mm_nt(
                b.d_hidden[i * LINE : (i + 1) * LINE, h * chan : (h + 1) * chan], v_of(h, low, n)
            )
            for k in range(n):
                b.score_part[h, at + k] = tile[:, k * LINE : (k + 1) * LINE]
    other = links.go(b.score_part.at[1 - m.core], b.score_in.at[0], m.sib)
    other.wait_recv()
    b.share_out[...] = (b.score_part[m.core] + b.score_in[0]).astype(BF)
    far = links.go(b.share_out, b.share_in, m.yn)
    far.wait_recv()
    b.lines[...] = jnp.zeros((8, rows), F32)
    for i, low, at, n in blocks:
        lines = slice(i * LINE, (i + 1) * LINE)
        across = slice(low * LINE, (low + n) * LINE)

        def spread(ref):
            return jnp.concatenate([ref[at + k].astype(F32) for k in range(n)], axis=1)

        inv, sign, radial = b.inv[lines][:, :1], b.sign[lines][:, :1], rho[lines]
        weight = spread(b.weight)
        full = (spread(b.share_out) + spread(b.share_in)) * inv - sign * radial * inv
        exact = jnp.where(sign == 0.0, radial, 0.0)
        noisy = jnp.sum(full * weight, axis=1, keepdims=True)
        square = jnp.sum(weight * weight, axis=1, keepdims=True)
        full = full - weight * ((noisy - exact) / jnp.where(square > 0.0, square, 1.0))
        d_score = (full * spread(b.decay)).astype(BF)
        for k in range(n):
            b.d_score[m.core, at + k] = d_score[:, k * LINE : (k + 1) * LINE]
        b.lines[0:1, across] += jnp.sum(full * weight, axis=0, keepdims=True)
        b.keep[lines] = jnp.broadcast_to(exact, (LINE, 128))
    next(gate_ticks)
    scored = links.go(b.d_score.at[m.core], b.d_score.at[m.core], m.sib)
    over_cols = b.lines[0:1]
    over_rows = b.keep[...].T[0:1]
    delta = jnp.broadcast_to(over_rows - over_cols, (8, rows))
    after = jnp.sum(delta, axis=1, keepdims=True) - prefix_lanes(delta) + delta
    forget = jnp.sum(jnp.where(line8 == head + all_heads, b.pre[...], 0.0), axis=0, keepdims=True)
    d_forget = after[:1] / (1.0 + jnp.exp(forget))
    own_lines = jnp.where(line8 == head, over_cols, 0.0) + jnp.where(
        line8 == head + all_heads, d_forget, 0.0
    )
    head_peers = [
        m.sib,
        m.xn,
        (m.z, m.sib_t, m.other_c),
    ]
    pre_sum = push_sum(links, m, own_lines, b.grad_box, head_peers, m.c * 2 + m.core, 4)

    for h in range(heads):
        at = slice(2 * local + h * chan, 2 * local + (h + 1) * chan)
        b.g_proj[:, at] = jnp.zeros((rows, chan), F32)
        for i, low, place, n in blocks:
            d_hid = b.d_hidden[i * LINE : (i + 1) * LINE, h * chan : (h + 1) * chan]
            b.g_proj[low * LINE : (low + n) * LINE, at] += mm_tn(wide(b.share, h, place, n), d_hid)
    next(gate_ticks)
    scored.wait_recv()
    for h in range(heads):
        at = slice(h * chan, (h + 1) * chan)
        k_at = slice(local + h * chan, local + (h + 1) * chan)
        b.g_proj[:, k_at] = jnp.zeros((rows, chan), F32)
        for i, low, place, n in blocks:
            tile = wide(b.d_score, h, place, n)
            b.g_proj[i * LINE : (i + 1) * LINE, at] = mm(tile, k_of(h, low, n))
            b.g_proj[low * LINE : (low + n) * LINE, k_at] += mm_tn(tile, q_of(h, i))
    pre_grad = pre_sum()
    next(gate_ticks)
    advance(1)
    pre16 = jnp.concatenate([pre_grad, jnp.zeros((8, rows), F32)], axis=0)
    high, rest = split(pre16)
    b.g_proj[...] += mm_tn(high, b.gates_w[...]) + mm_tn(rest, b.gates_w[...])
    gate_grad = (mm(high, b.qkv[...]) + mm(rest, b.qkv[...]))[:8]
    for s in range(3):
        b.low_sum[8 * s : 8 * (s + 1)] = gate_grad[:, s * local : (s + 1) * local]
    bias_grad = jnp.sum(pre_grad, axis=1, keepdims=True)
    b.small[7:8, wide_d : wide_d + 128] = to_lanes_one(bias_grad)
    advance(2)

    r_map = lax.broadcasted_iota(jnp.int32, (chan, chan), 0) // 4
    c_map = lax.broadcasted_iota(jnp.int32, (chan, chan), 1) // 4
    same = r_map == c_map
    for h in range(heads):
        at = slice(h * chan, (h + 1) * chan)
        act_low = b.act[:, at].astype(BF)
        extra = None
        for s in range(3):
            low = b.g_proj[:, s * local + h * chan : s * local + (h + 1) * chan].astype(BF)
            left = act_low if s < 2 else b.branch[:, at]
            dense = jnp.where(same, mm_tn(left, low), 0.0)
            folded = jnp.sum(dense.reshape(chan // 8, 8, chan), axis=0)
            b.low_sum[24 + 4 * s : 28 + 4 * s, at] = folded[:4] + folded[4:]
            back = mm_nt(low, b.maps[s, h])
            if s == 0:
                extra = back
            elif s == 1:
                b.g_act[:, at] += extra + back
            else:
                b.wide_f[:, at] = back

    def unconvolve(i, carry):
        at = pl.ds(pl.multiple_of(i * 128, 128), 128)
        since = lax.broadcasted_iota(jnp.int32, (rows, 128), 0) - b.begin[...]
        x = b.branch[:, at].astype(F32)
        gc = b.g_act[:, at] * b.slope[:, at]
        gb = b.wide_f[:, at] + b.chan_params[0:1, at] * gc
        b.small[0:1, at] = jnp.sum(gc * x, axis=0, keepdims=True)
        b.small[4:5, at] = jnp.sum(gc, axis=0, keepdims=True)
        for j in range(1, 4):
            kept = jnp.where(since >= j, gc, 0.0)
            gb = gb + b.chan_params[j : j + 1, at] * pltpu.roll(kept, rows - j, 0)
            b.small[j : j + 1, at] = jnp.sum(kept * pltpu.roll(x, j, 0), axis=0, keepdims=True)
        b.g_cell[:, at] = gb.astype(BF)
        return carry

    lax.fori_loop(0, local // 128, unconvolve, 0)
    next(gate_ticks)
    next(cell_ticks)
    next(cell_ticks)
    b.low_sum[36:] = jnp.zeros((12, local), F32)
    b.low_box[m.z] = b.low_sum[...].astype(BF)
    low_copies = [links.go(b.low_box.at[m.z], b.low_box.at[m.z], peer) for peer in m.dp_peers]
    advance(4)

    def up_part(y, core, x):
        slot = (y * 2 + core) * 2 + x
        if block >= wide_d:
            ratio = block // wide_d
            at = pl.ds(pl.multiple_of(lax.rem(slot, ratio) * wide_d, 16), wide_d)
            owner = lax.div(slot, ratio)
            return mm_nt(b.g_cell[...], b.up_cell[owner, at]) + mm_nt(
                b.g_gate[...], b.up_gate[owner, at]
            )
        ratio = wide_d // block
        return jnp.concatenate(
            [
                mm_nt(b.g_cell[...], b.up_cell[slot * ratio + k])
                + mm_nt(b.g_gate[...], b.up_gate[slot * ratio + k])
                for k in range(ratio)
            ],
            axis=1,
        )

    own_k = m.y * 2 + m.c
    services = (lambda: advance(2), tick(gate_ticks), tick(gate_ticks))
    for _ in plane_scatter(links, m, up_part, b, rows, services):
        pass
    for _ in gate_ticks:
        pass
    grad_normed = b.acc[own_k]
    x_hat = (b.x_own[...].astype(F32) - b.sums[:, :1]) * b.squares[:, :1]
    grad_scaled = grad_normed * b.gains[m.slot, :1]
    line_sum = push_sum(
        links,
        m,
        to_lanes(
            [
                jnp.sum(grad_scaled, axis=1, keepdims=True),
                jnp.sum(grad_scaled * x_hat, axis=1, keepdims=True),
            ],
            rows,
        ),
        b.line_box,
        m.plane_peers,
        m.slot,
        8,
    )
    loss_sum = push_sum(links, m, b.loss_part[...], b.loss_box, m.plane_peers, m.slot, 8)
    b.small[7:8, :wide_d] = jnp.sum(grad_normed * x_hat, axis=0, keepdims=True)
    b.small[7:8, wide_d + 128 :] = loss_sum()[:1]
    b.small_box[m.z] = b.small[...]
    small_copies = [
        links.go(b.small_box.at[m.z], b.small_box.at[m.z], peer) for peer in m.dp_peers
    ]
    next(cell_ticks)
    lines = to_columns(line_sum()) / width
    grad_x = b.squares[:, :1] * (grad_scaled - lines[:, :1] - x_hat * lines[:, 1:2])
    own_grad = b.own_gradient[...].astype(F32)
    grad_slot = (own_grad + grad_x).astype(BF)
    links.settle(b.token_copies)
    b.sent_tokens[...] = mm_tn(b.recv_map[...], grad_slot).astype(BF)
    own_place = pl.ds(pl.multiple_of(m.z * cap, 16), cap)
    b.home_grad[own_place] = b.sent_tokens[own_place]
    copies = b.exchange(b.sent_tokens, b.home_grad)
    next(cell_ticks)
    for copy in b.home_copies:
        copy.wait_recv()
    b.output[...] = mm_tn(b.send_map[...], b.home_out[...]).astype(BF)
    next(cell_ticks)
    advance(3)
    for copy in small_copies + low_copies:
        copy.wait_recv()
    lows = b.low_box[0].astype(F32)
    for k in range(1, n_dp):
        lows = lows + b.low_box[k].astype(F32)
    b.low_sum[...] = lows
    total = b.small_box[0]
    for k in range(1, n_dp):
        total = total + b.small_box[k]
    b.small[...] = total
    b.loss[...] = total[7:8, wide_d + 128 : wide_d + 129]
    b.grad_ln[...] = total[7:8, :wide_d]
    for h in range(heads):
        at = slice(h * chan, (h + 1) * chan)
        for j in range(4):
            b.grad_conv_weight[j, h : h + 1] = b.small[j : j + 1, at]
        for j, ref in ((4, b.grad_conv_bias), (5, b.grad_group), (6, b.grad_skip)):
            ref[h : h + 1] = b.small[j : j + 1, at]
        for s in range(3):
            for i in range(4):
                k = 24 + 4 * s + i
                b.grad_qkv[s, i, h : h + 1] = b.low_sum[k : k + 1, at]
            for g in range(2 * all_heads):
                k = 8 * s + g
                b.grad_gate_weight[g // all_heads, g % all_heads, s, h : h + 1] = b.low_sum[
                    k : k + 1, at
                ]
    for g in range(2):
        at = wide_d + g * all_heads
        b.grad_gate_bias[g : g + 1] = total[7:8, at : at + all_heads]
    for _ in cell_ticks:
        pass
    for copy in copies:
        copy.wait_recv()
    b.grad_input[...] = mm_tn(b.send_map[...], b.home_grad[...]).astype(BF)
    for line in [b.mixed_ring] + gates + cells:
        line.settle()


def kernel(names, shape, limit, *refs):
    b = types.SimpleNamespace(**dict(zip(names, refs)))
    m = coordinates(shape[3])
    links = Links(b.send_sem, b.recv_sem, limit)
    forward(b, m, links, shape)
    backward(b, m, links, shape)
    links.close()


def carry_out(*refs):
    *ends, sems = refs
    half = len(ends) // 2
    copies = [
        pltpu.make_async_copy(ends[k], ends[half + k], sems.at[k]) for k in range(half)
    ]
    for copy in copies:
        copy.start()
    for copy in copies:
        copy.wait()


def shards(
    tokens,
    targets,
    ln_gain,
    up_weight,
    conv_weight,
    conv_bias,
    qkv_weight,
    gate_weight,
    gate_bias,
    group_gain,
    skip_gain,
    down_weight,
    lengths,
    permutation,
    valid,
):
    rows, wide_d = tokens.shape
    n_dp = lax.axis_size("dp")
    heads, chan = up_weight.shape[2], up_weight.shape[3]
    local = heads * chan
    block = up_weight.shape[0]
    width = 8 * wide_d
    up_halves = up_weight.transpose(1, 0, 2, 3).reshape(2, block, local)
    inputs = dict(
        tokens=tokens,
        targets=targets,
        permutation=permutation,
        valid=valid,
        own_cell=up_halves[0],
        own_gate=up_halves[1],
        own_down=down_weight.reshape(local, block),
        ln_gain=ln_gain,
        conv_weight=conv_weight,
        conv_bias=conv_bias,
        qkv_weight=qkv_weight,
        gate_weight=gate_weight,
        gate_bias=gate_bias,
        group_gain=group_gain,
        skip_gain=skip_gain,
        lengths=lengths,
    )
    outputs = dict(
        output=((rows, wide_d), BF),
        loss=((1, 1), F32),
        grad_input=((rows, wide_d), BF),
        grad_ln=((1, wide_d), F32),
        grad_up=(up_weight.shape, F32),
        grad_conv_weight=(conv_weight.shape, F32),
        grad_conv_bias=(conv_bias.shape, F32),
        grad_qkv=(qkv_weight.shape, F32),
        grad_gate_weight=(gate_weight.shape, F32),
        grad_gate_bias=(gate_bias.shape, F32),
        grad_group=(group_gain.shape, F32),
        grad_skip=(skip_gain.shape, F32),
        grad_down=((local, block), F32),
    )
    n_blocks = band(rows)[1]
    half = rows // 2
    limit = 150 + 14 * n_dp
    turns = (2 if n_dp <= 4 else 1, n_dp)
    scratch = dict(
        send_map=((rows, rows), BF),
        recv_map=((rows, rows), BF),
        chan_params=((8, local), F32),
        maps8=((3, heads, 8, chan), F32),
        gates_f=((16, 3 * local), F32),
        gates_w=((16, 3 * local), BF),
        sent_tokens=((rows, wide_d), BF),
        sent_goal=((rows, wide_d), BF),
        goal_places=((rows, wide_d), BF),
        valids=((n_dp, 8, rows), F32),
        keep=((rows, 128), F32),
        full=((8, rows, wide_d), BF),
        gains=((8, 8, wide_d), F32),
        up_cell=((n_dp, block, local), BF),
        up_gate=((n_dp, block, local), BF),
        down=((n_dp, local, block), BF),
        sums=((rows, 128), F32),
        squares=((rows, 128), F32),
        x_own=((rows, wide_d), BF),
        normed=((rows, width), BF),
        wide_f=((rows, local), F32),
        begin=((rows, 128), jnp.int32),
        branch=((rows, local), BF),
        act=((rows, local), F32),
        slope=((rows, local), F32),
        maps=((3, heads, chan, chan), BF),
        qkv=((rows, 3 * local), BF),
        pre_box=((8, 8, rows), F32),
        pre=((8, rows), F32),
        score_part=((heads, n_blocks, LINE, LINE), F32),
        score_in=((2, n_blocks, LINE, LINE), F32),
        score_sum=((n_blocks, LINE, LINE), F32),
        decay=((n_blocks, LINE, LINE), F32),
        weight=((n_blocks, LINE, LINE), F32),
        share=((heads, n_blocks, LINE, LINE), BF),
        inv=((rows, 128), F32),
        sign=((rows, 128), F32),
        hidden=((rows, local), F32),
        moment_box=((4, 8, rows), F32),
        head_rstd=((heads, rows, 128), F32),
        head_mean=((heads, rows, 128), F32),
        gate_low=((rows, local), BF),
        out=((4, rows, wide_d), BF),
        into=((4, rows, wide_d), BF),
        acc=((4, rows, wide_d), F32),
        small_out=((6 * GROUPS, half // GROUPS, wide_d), BF),
        small_in=((6 * GROUPS, half // GROUPS, wide_d), BF),
        loss_part=((8, 128), F32),
        goal=((rows, wide_d), BF),
        result=((rows, wide_d), BF),
        own_gradient=((rows, wide_d), BF),
        sent_out=((rows, wide_d), BF),
        home_out=((rows, wide_d), BF),
        home_grad=((rows, wide_d), BF),
        mixed_all=((n_dp, rows, local), BF),
        cols_out=((n_dp, rows // 8, block), BF),
        cols=((8, n_dp * rows // 8, block), BF),
        low_sum=((48, local), F32),
        low_box=((n_dp, 48, local), BF),
        ring_gate=((heads,) + turns + (block, chan), BF),
        ring_cell=((heads,) + turns + (block, chan), BF),
        g_gate=((rows, local), BF),
        g_cell=((rows, local), BF),
        small=((8, local), F32),
        small_box=((n_dp, 8, local), F32),
        g_act=((rows, local), F32),
        u_box=((4, 8, rows), F32),
        d_hidden=((rows, local), BF),
        share_out=((n_blocks, LINE, LINE), BF),
        share_in=((n_blocks, LINE, LINE), BF),
        lines=((8, rows), F32),
        d_score=((heads, n_blocks, LINE, LINE), BF),
        grad_box=((4, 8, rows), F32),
        g_proj=((rows, 3 * local), F32),
        line_box=((8, 8, rows), F32),
        loss_box=((8, 8, 128), F32),
    )
    vmem = pl.BlockSpec(memory_space=pltpu.VMEM)
    spaces = {name: pl.BlockSpec(memory_space=pl.ANY) for name in inputs if name[:4] == "own_"}
    spaces["lengths"] = pl.BlockSpec(memory_space=pltpu.SMEM)
    names = list(inputs) + list(outputs) + list(scratch) + ["send_sem", "recv_sem", "local_sem"]
    results = pl.pallas_call(
        lambda *refs: kernel(names, (rows, local, chan, n_dp, block, wide_d), limit, *refs),
        out_shape=[jax.ShapeDtypeStruct(*spec) for spec in outputs.values()],
        in_specs=[spaces.get(name, vmem) for name in inputs],
        out_specs=[vmem] * len(outputs),
        scratch_shapes=[pltpu.VMEM(*spec) for spec in scratch.values()]
        + [pltpu.SemaphoreType.DMA((limit,)), pltpu.SemaphoreType.DMA((limit,))]
        + [pltpu.SemaphoreType.DMA((3,))],
        compiler_params=pltpu.CompilerParams(
            collective_id=0, has_side_effects=True, vmem_limit_bytes=VMEM_LIMIT
        ),
    )(*inputs.values())
    results = pl.pallas_call(
        carry_out,
        out_shape=[jax.ShapeDtypeStruct(*spec) for spec in outputs.values()],
        in_specs=[pl.BlockSpec(memory_space=pl.ANY)] * len(outputs),
        out_specs=[vmem] * len(outputs),
        scratch_shapes=[pltpu.SemaphoreType.DMA((len(outputs),))],
    )(*results)
    o = types.SimpleNamespace(**dict(zip(outputs, results)))
    return (
        o.output,
        o.loss.reshape(()),
        o.grad_input,
        o.grad_ln.reshape(-1),
        o.grad_up,
        o.grad_conv_weight,
        o.grad_conv_bias,
        o.grad_qkv,
        o.grad_gate_weight,
        o.grad_gate_bias,
        o.grad_group,
        o.grad_skip,
        o.grad_down.reshape(down_weight.shape),
    )


def solution(mesh):
    return jax.shard_map(
        shards,
        mesh=mesh,
        in_specs=(
            P("dp", ("tensor", "ctx")),
            P("dp", ("tensor", "ctx")),
            P(("tensor", "ctx")),
            P("dp", None, "ctx", "tensor"),
            P(None, "ctx", "tensor"),
            P("ctx", "tensor"),
            P(None, None, "ctx", "tensor"),
            P(None, None, None, "ctx", "tensor"),
            P(),
            P("ctx", "tensor"),
            P("ctx", "tensor"),
            P("ctx", "tensor", "dp"),
            P(),
            P(),
            P("dp"),
        ),
        out_specs=(
            P("dp", ("tensor", "ctx")),
            P(),
            P("dp", ("tensor", "ctx")),
            P(("tensor", "ctx")),
            P("dp", None, "ctx", "tensor"),
            P(None, "ctx", "tensor"),
            P("ctx", "tensor"),
            P(None, None, "ctx", "tensor"),
            P(None, None, None, "ctx", "tensor"),
            P(),
            P("ctx", "tensor"),
            P("ctx", "tensor"),
            P("ctx", "tensor", "dp"),
        ),
        check_vma=False,
    )
```

profile of v0, /device:TPU:0, one launch (start us, length us, event | category | flops | bytes accessed | tf_op | source)
XLA Modules:
  0.0 256.6 jit_solution(6534313789805225492)
XLA Ops:
  0.6 1.9 fusion
  2.6 0.9 copy.29
  3.5 0.9 copy.28
  4.3 247.3 %shard_map.246 = (bf16[512,256]{1,0:T(8,128)(2,1)}, f32[1,1]{1,0:T(1,128)}, bf16[512,256]{1,0:T(8,128)(2,1)}, f32[1,256]{1,0:T(1,128)}, f32[512,2,2,256]{3,2,1,0...) custom-call(bf16[512,256]{1,0:T(8,128)(2,1)} %refs_0_.1, ...), custom_call_target="tpu_custom_call" | custom-call | tf_op jit(solution)/shard_map/pallas_call | solution.py:1406
  251.7 4.7 %shard_map.247 = (bf16[512,256]{1,0:T(8,128)(2,1)}, f32[1,1]{1,0:T(1,128)}, bf16[512,256]{1,0:T(8,128)(2,1)}, f32[1,256]{1,0:T(1,128)}, f32[512,2,2,256]{3,2,1,0...) custom-call(bf16[512,256]{1,0:T(8,128)(2,1)} %get-tuple-element.39.r, ...), custom_call_target="tpu_custom_call" | custom-call | tf_op jit(solution)/shard_map/pallas_call | solution.py:1418
where the time goes:
time: 259 us; the launch traced here: 257 us
  Pallas kernels  252 us (97%)
  local copies, waits for them, and re-layouts  3.68 us (1%)
    pallas_call x1, Pallas kernels, shards(): pl.pallas_call(lambda *refs: kernel(names, (rows, local, chan, n_dp, bloc...  247 us

commit v1 on v0

--- a/solution.py
+++ b/solution.py
@@ -940,7 +940,7 @@
 
     def up_ring(grads, hold, g, h):
         at_h = slice(h * chan, (h + 1) * chan)
-        size = block // 2 if g else block
+        size = block // 2 if g and h else block
 
         def part(owner, j=None):
             if j is None:

time: 259 us -> 258 us (level)
  no operation moved by 1% of the time
where the time goes in v1:
time: 258 us; the launch traced here: 256 us
  Pallas kernels  251 us (97%)
  local copies, waits for them, and re-layouts  3.68 us (1%)
    pallas_call x1, Pallas kernels, shards(): pl.pallas_call(lambda *refs: kernel(names, (rows, local, chan, n_dp, bloc...  247 us

profile of v1, /device:TPU:0, one launch (start us, length us, event | category | flops | bytes accessed | tf_op | source)
XLA Modules:
  0.0 255.9 jit_solution(6423617010335847700)
XLA Ops:
  0.6 1.9 fusion
  2.6 0.9 copy.29
  3.5 0.9 copy.28
  4.3 246.6 %shard_map.246 = (bf16[512,256]{1,0:T(8,128)(2,1)}, f32[1,1]{1,0:T(1,128)}, bf16[512,256]{1,0:T(8,128)(2,1)}, f32[1,256]{1,0:T(1,128)}, f32[512,2,2,256]{3,2,1,0...) custom-call(bf16[512,256]{1,0:T(8,128)(2,1)} %refs_0_.1, ...), custom_call_target="tpu_custom_call" | custom-call | tf_op jit(solution)/shard_map/pallas_call | solution.py:1406
  251.0 4.7 %shard_map.247 = (bf16[512,256]{1,0:T(8,128)(2,1)}, f32[1,1]{1,0:T(1,128)}, bf16[512,256]{1,0:T(8,128)(2,1)}, f32[1,256]{1,0:T(1,128)}, f32[512,2,2,256]{3,2,1,0...) custom-call(bf16[512,256]{1,0:T(8,128)(2,1)} %get-tuple-element.39.r, ...), custom_call_target="tpu_custom_call" | custom-call | tf_op jit(solution)/shard_map/pallas_call | solution.py:1418
